TPU v7x, 32 devices: a whole 2x2x4 slice. The times are simulated.
32 devices in a mesh: groups: 2 (over y), seq: 4 (over z), head: 2 (over x), sub: 2 (over core).
Axes of the slice: x: 2, y: 2, z: 4, core: 2. Of those that a mesh axis runs over, the one named last changes fastest.
Arguments:
- x_raw: bfloat16 [16, 128, 8192], P(('groups', 'seq', 'sub'), 'head'), parts along dimension 0, may hold values from -6 to 6
- bc_raw: bfloat16 [16, 128, 2048], P(('groups', 'seq', 'sub'), 'head'), parts along dimension 0, may hold values from -6 to 6
- dt_raw: bfloat16 [16, 128, 128], P(('groups', 'seq', 'sub'), 'head'), parts along dimension 0, may hold values from -3 to 40
- conv_x_weight: float32 [4, 8192], P(None, 'head'), may hold values from -3 to 3
- conv_x_bias: float32 [8192], P('head'), may hold values from -2.5 to 2.5
- conv_bc_weight: float32 [4, 2048], P(None, 'head'), may hold values from -3 to 3
- conv_bc_bias: float32 [2048], P('head'), may hold values from -2.5 to 2.5
- stride_offset_per_head: float32 [128], P('head'), may hold values from -12 to 0
- a_log: float32 [128], P('head'), may hold values from -8 to 3
- skip_d: float32 [128], P('head'), may hold values from 0.5 to 1.5
- norm_gain: float32 [8192], P('head'), may hold values from 0.1 to 1.9
Outputs:
- mixed: bfloat16 [16, 128, 8192], P(('groups', 'seq', 'sub'), None, 'head'), parts along dimension 0
There are 2 independent parts, one for each index of `groups`. A program takes and returns all parts, laid end to end along the dimension named above; an argument that names none is the same for every part. Nothing has to cross between parts.
All inputs are finite; a program needn't handle non-finite values.
Results may differ from a plain program's by a relative error of at most 0.0061.
Values may be sent and summed in bfloat16 or wider, within the bound.
A program may use at most 128 MiB of HBM per device.

v0:
```python
import jax
import jax.numpy as jnp
from jax import lax
from jax.sharding import PartitionSpec as P

STATE = 128
SPAN = 128


NORM_EPSILON = 1e-05


def shifted(value, axis, steps):
    count = lax.axis_size(axis)
    leading, last = (max(0, -steps), min(count, count - steps))
    return lax.ppermute(value, axis, [(source, source + steps) for source in range(leading, last)])


def from_partner(shard, axis, distance):
    return lax.ppermute(shard, axis, [(i, i ^ 1 << distance) for i in range(lax.axis_size(axis))])


def prefix_2(shard, axis, combine, identity):
    length, position = (lax.axis_size(axis), lax.axis_index(axis))
    everything = jax.tree.map(lambda part: lax.all_gather(part, axis), shard)
    start = jax.tree.map(
        lambda part, zero: jnp.broadcast_to(jnp.asarray(zero, part.dtype), part.shape),
        shard,
        identity,
    )

    def hop(k, before):
        reached = k < position
        new = combine(before, jax.tree.map(lambda part: part[k], everything))
        return jax.tree.map(lambda a, b: jnp.where(reached, a, b), new, before)

    return lax.fori_loop(0, length, hop, start)


def conv_rows(raw_rows, rim_rows, weight, bias):
    conv_width = weight.shape[0]
    row_count = raw_rows.shape[0]
    joined = jnp.concatenate([rim_rows, raw_rows], axis=0).astype(jnp.float32)
    running = bias[None, :]
    for tap_index in range(conv_width):
        running = running + weight[tap_index][None, :] * joined[tap_index : tap_index + row_count]
    return jax.nn.silu(running).astype(jnp.bfloat16)


def chain_step(earlier, later_part):
    decay_early, state_early = earlier
    decay_later, state_later = later_part
    return (decay_early * decay_later, decay_later[..., None] * state_early + state_later)


def on_device(
    x_raw,
    bc_raw,
    dt_raw,
    conv_x_weight,
    conv_x_bias,
    conv_bc_weight,
    conv_bc_bias,
    stride_offset_per_head,
    a_log,
    skip_d,
    norm_gain,
):
    x_ex, bc_ex, dt_ex = (
        lax.all_to_all(x_raw, "head", split_axis=2, concat_axis=1, tiled=True),
        lax.all_to_all(bc_raw, "head", split_axis=2, concat_axis=1, tiled=True),
        lax.all_to_all(dt_raw, "head", split_axis=2, concat_axis=1, tiled=True),
    )
    x_rows = x_ex[0]
    bc_rows = bc_ex[0]
    dt_rows = dt_ex[0]
    conv_width = conv_x_weight.shape[0]
    x_rim, bc_rim = shifted(
        (x_rows[x_rows.shape[0] - conv_width + 1 :], bc_rows[bc_rows.shape[0] - conv_width + 1 :]),
        ("seq", "sub"),
        1,
    )
    x_conv = conv_rows(x_rows, x_rim, conv_x_weight, conv_x_bias)
    bc_conv = conv_rows(bc_rows, bc_rim, conv_bc_weight, conv_bc_bias)
    row_count = x_conv.shape[0]
    head_count = dt_rows.shape[1]
    groups = bc_conv.shape[1] // (2 * STATE)
    per_group = head_count // groups
    head_dim = x_conv.shape[1] // head_count
    group_width = per_group * head_dim
    span_len = SPAN
    blocks = row_count // span_len
    dt_step = jax.nn.softplus(dt_rows.astype(jnp.float32) + stride_offset_per_head[None, :])
    decay_rate = -jnp.exp(a_log)
    decay_logarithm_rows = (decay_rate[None, :] * dt_step).reshape(blocks, span_len, head_count)
    cum_decay = jnp.cumsum(decay_logarithm_rows, axis=1)
    step_blocks = dt_step.reshape(blocks, span_len, head_count)
    x_blocks = x_conv.reshape(blocks, span_len, groups, per_group, head_dim)
    x_wide = x_conv.reshape(blocks, span_len, groups, group_width)
    bc_blocks = bc_conv.reshape(blocks, span_len, groups, 2, STATE)
    b_in = bc_blocks[:, :, :, 0]
    c_out = bc_blocks[:, :, :, 1]

    def widen(per_head):
        return jnp.repeat(per_head, head_dim, axis=-1).reshape(
            per_head.shape[:-1] + (groups, group_width)
        )

    causal = lax.broadcasted_iota(jnp.int32, (span_len, span_len), 0) >= lax.broadcasted_iota(
        jnp.int32, (span_len, span_len), 1
    )
    inner_prod = jnp.einsum("btgn,bsgn->bgts", c_out, b_in, preferred_element_type=jnp.float32)
    cum_heads = jnp.transpose(cum_decay, (0, 2, 1)).reshape(blocks, groups, per_group, span_len)
    step_heads = jnp.transpose(step_blocks, (0, 2, 1)).reshape(blocks, groups, per_group, span_len)
    gap_pairs = cum_heads[..., :, None] - cum_heads[..., None, :]
    weight = jnp.exp(jnp.where(causal, gap_pairs, -1e30)) * step_heads[..., None, :]
    mixing = (inner_prod[:, :, None] * weight).astype(jnp.bfloat16)
    within_block_output = jnp.einsum(
        "bgjts,bsgjp->btgjp", mixing, x_blocks, preferred_element_type=jnp.float32
    )
    within_wide = within_block_output.reshape(blocks, span_len, groups, group_width)
    block_end = cum_decay[:, span_len - 1 :, :]
    to_end = jnp.exp(block_end - cum_decay) * step_blocks
    scaled = (widen(to_end) * x_wide).astype(jnp.bfloat16)
    states = jnp.einsum("bsgq,bsgn->bgqn", scaled, b_in, preferred_element_type=jnp.float32)
    decays = widen(jnp.exp(block_end[:, 0, :]))
    identity = (
        jnp.ones((groups, group_width), jnp.float32),
        jnp.zeros((groups, group_width, STATE), jnp.float32),
    )

    def local_step(running, block_item):
        return (chain_step(running, block_item), running)

    own_part, prefix = lax.scan(local_step, identity, (decays, states))
    partner = from_partner((own_part[0], own_part[1]), "sub", 0)
    is_lower = lax.axis_index("sub") == 0
    first_part = jax.tree.map(
        lambda mine, other: jnp.where(is_lower, mine, other), own_part, partner
    )
    second_part = jax.tree.map(
        lambda mine, other: jnp.where(is_lower, other, mine), own_part, partner
    )
    pair_total = chain_step(first_part, second_part)
    before_pair = prefix_2(pair_total, "seq", chain_step, identity)
    inside_pair = jax.tree.map(
        lambda empty, other: jnp.where(is_lower, empty, other), identity, partner
    )
    entry_part = chain_step(before_pair, inside_pair)
    device_entry = entry_part[1]
    carried = prefix[0][..., None] * device_entry[None] + prefix[1]
    carried_bf = carried.astype(jnp.bfloat16)
    y_state = jnp.einsum("btgn,bgqn->btgq", c_out, carried_bf, preferred_element_type=jnp.float32)
    y_state = y_state * widen(jnp.exp(cum_decay))
    skip_wide = jnp.repeat(skip_d, head_dim).reshape(groups, group_width)
    complete_output = within_wide + y_state + skip_wide * x_wide
    squares_mean = jnp.mean(complete_output * complete_output, axis=3)
    normed = (
        complete_output
        * lax.rsqrt(squares_mean + NORM_EPSILON)[..., None]
        * norm_gain.reshape(groups, group_width)
    )
    return normed.reshape(row_count, head_count * head_dim).astype(jnp.bfloat16)[None]


def solution(mesh):
    placed = (
        P(("groups", "seq", "sub"), "head", None),
        P(("groups", "seq", "sub"), "head", None),
        P(("groups", "seq", "sub"), "head", None),
        P(None, "head"),
        P("head"),
        P(None, "head"),
        P("head"),
        P("head"),
        P("head"),
        P("head"),
        P("head"),
    )
    return jax.shard_map(
        on_device,
        mesh=mesh,
        in_specs=placed,
        out_specs=P(("groups", "seq", "sub"), None, "head"),
        check_vma=False,
    )
```

profile of v0, /device:TPU:29, one launch (start us, length us, event | category | flops | bytes accessed | tf_op | source)
XLA Modules:
  0.0 311.8 jit_solution(2477985931013234938)
XLA Ops:
  6.5 0.8 copy.58
  8.0 0.9 reduce.6
  8.8 0.7 reshape.322
  9.6 3.2 %all-to-all-start.2 = ((bf16[2,2,2048]{2,1,0:T(2,128)(2,1)}), bf16[2,2,2048]{2,1,0:T(2,128)(2,1)S(1)}, u32[]{:S(2)}, u32[]{:S(2)}) async-start(bf16[2,2,2048]{2,1,0:T(2,128)(2,1)} %reshape.322), calls=%async_computation.2 | async-start | bytes 32768 | tf_op jit(solution)/shard_map/all_to_all | solution.py:72
  12.8 1.7 fusion.27
  14.5 0.9 fusion.28
  16.0 9.2 %copy.48 = bf16[1,64,8192]{1,0,2:T(2,128)(2,1)} copy(bf16[1,64,8192]{2,1,0:T(8,128)(2,1)} %param.13) | data formatting | bytes 2097152 | tf_op args[0]
  25.2 45.3 %reduce.5 = bf16[8192,64]{1,0:T(8,128)(2,1)S(1)} reduce(bf16[8192,1,64]{2,1,0:T(2,128)(2,1)} %bitcast.99, bf16[]{:T(256)} %broadcast.182), dimensions={1}, to_apply=%bitcast.80.reduce_sub_computation | reduce | bytes 2097154
  70.5 2.4 reshape.320
  72.9 0.7 copy.52
  73.7 11.8 %reduce.7 = bf16[2048,64]{1,0:T(8,128)(2,1)S(1)} reduce(bf16[2048,1,64]{2,1,0:T(2,128)(2,1)S(1)} %bitcast.106, bf16[]{:T(256)} %broadcast.182), dimensions={1}, to_apply=%bitcast.84.reduce_sub_computation | reduce | bytes 524290
  85.4 1.1 reshape.324
  86.5 3.4 %all-to-all-start.1 = ((bf16[2,2,32768]{2,1,0:T(2,128)(2,1)}), bf16[2,2,32768]{2,1,0:T(2,128)(2,1)S(1)}, u32[]{:S(2)}, u32[]{:S(2)}) async-start(bf16[2,2,32768]{2,1,0:T(2,128)(2,1)} %reshape.324), calls=%async_computation.1 | async-start | bytes 524288 | tf_op jit(solution)/shard_map/all_to_all | solution.py:71
  90.3 0.7 broadcast_multiply_fusion
  91.6 0.7 collective-permute-start.2
  92.3 2.2 all-to-all-done.1
  94.5 3.6 %all-to-all-start = ((bf16[2,2,131072]{2,1,0:T(2,128)(2,1)}), bf16[2,2,131072]{2,1,0:T(2,128)(2,1)S(1)}, u32[]{:S(2)}, u32[]{:S(2)}) async-start(bf16[2,2,131072]{2,1,0:T(2,128)(2,1)} %reshape.320), calls=%async_computation | async-start | bytes 2097152 | tf_op jit(solution)/shard_map/all_to_all | solution.py:70
  100.3 1.3 collective-permute-start.1
  102.2 2.2 collective-permute-done.1
  104.4 5.7 %all-to-all-done = bf16[2,2,131072]{2,1,0:T(2,128)(2,1)S(1)} async-done(((bf16[2,2,131072]{2,1,0:T(2,128)(2,1)}), bf16[2,2,131072]{2,1,0:T(2,128)(2,1)S(1)}, u32[]{:S(2)}, u32[]{:S(2)}) %all-to-all-start) | async-done | bytes 1048608 | tf_op jit(solution)/shard_map/all_to_all | solution.py:70
  110.2 2.7 reshape.321
  112.9 8.2 %copy.49 = bf16[1,64,8192]{2,1,0:T(8,128)(2,1)S(1)} copy(bf16[1,64,8192]{1,0,2:T(2,128)(2,1)} %bitcast.98) | data formatting | bytes 2097152 | tf_op jit(solution)/shard_map/all_to_all | solution.py:70
  121.1 0.8 all_to_all.30
  122.5 1.3 collective-permute-start
  124.4 3.2 %collective-permute-done = bf16[3,4096]{1,0:T(4,128)(2,1)S(1)} collective-permute-done((bf16[3,4096]{1,0:T(4,128)(2,1)S(1)}, bf16[3,4096]{1,0:T(4,128)(2,1)S(1)}, u32[]{:S(2)}, u32[]{:S(2)}) %collective-permute-start) | collective-permute-done | bytes 24608 | tf_op jit(solution)/shard_map/ppermute | solution.py:16
  128.0 1.3 multiply_convert_fusion.3
  129.8 0.9 broadcast_in_dim.66
  131.5 0.8 convolution_add_fusion
  132.2 2.7 collective-permute-start.3
  134.9 3.8 %collective-permute-done.3 = f32[4,1024,128]{2,1,0:T(8,128)S(1)} collective-permute-done((f32[4,1024,128]{2,1,0:T(8,128)S(1)}, f32[4,1024,128]{2,1,0:T(8,128)S(1)}, u32[]{:S(2)}, u32[]{:S(2)}) %collective-permute-start.3) | collective-permute-done | bytes 2097184 | tf_op jit(solution)/shard_map/ppermute | solution.py:20
  138.7 1.3 copy-done.2
  140.1 1.7 select_add_fusion
  143.1 0.8 broadcast_in_dim.72
  144.0 1.3 mul.290
  147.3 18.3 %all-gather.2 = f32[4,4,1024]{2,1,0:T(4,128)S(1)} all-gather(f32[1,4,1024]{2,1,0:T(4,128)} %get-tuple-element.160), channel_id=2, replica_groups=mesh['groups'=2,'seq'=4,'head'=2,'sub'=2] {'seq'}, dimensions={0}, use_global_device_ids=true | all-gather | bytes 81920 | tf_op jit(solution)/shard_map/all_gather | solution.py:25
  165.6 0.9 fusion.22
  166.5 1.3 copy.51
  167.8 3.9 %fusion.1 = f32[4,16,64,128]{3,2,1,0:T(8,128)} fusion(bf16[128,4,16,64]{0,3,2,1:T(8,128)(2,1)} %bitcast.114, f32[4,16,128]{2,1,0:T(8,128)S(1)} %bitcast.124, f32[4,16,128]{2,1,0:T(8,128)S(1)} %bitcast.125, f32[4,128,128]{2,1,0:T(8,128)} %fusion.22, pred[128,128]{1,0:T(8,128)(4,1)} %iota_compare_fusion), kind=kOutput, calls=%fused_computation.4 | convolution fusion | flops 139460608 | bytes 3489792 | tf_op jit(solution)/shard_map/bgjts,bsgjp->btgjp/dot_general | solution.py:118
  171.7 117.8 %all-gather.5.cloned.1.call-done = f32[16,1024,128]{2,1,0:T(8,128)} async-done(((f32[4,1024,128]{2,1,0:T(8,128)}), f32[16,1024,128]{2,1,0:T(8,128)}) %all-gather.5.cloned.1.call-update) | async-done | bytes 8388624 | tf_op jit(solution)/shard_map/all_gather | solution.py:25
  289.6 8.8 %while.9 = (s32[]{:T(128)}, f32[4,1024,128]{2,1,0:T(8,128)S(1)}, s32[]{:T(128)}, f32[4,4,1024]{2,1,0:T(4,128)S(1)}, f32[4,4,1024,128]{3,2,1,0:T(8,128)}, /*index=5*/s32[]{:T(128)}, s32[]{:T(128)}) while((s32[]{:T(128)}, f32[4,1024,128]{2,1,0:T(8,128)S(1)}, s32[]{:T(128)}, f32[4,4,1024]{2,1,0:T(4,128)S(1)}, ...), condition=%wide.region_2.3_spmd.clone, body=%wide.region_1.2_spmd.clone.sunk | while | flops 2097156 | bytes 6340713 | solution.py:37
  289.6 2.2 fusion.32
  291.8 2.2 fusion.32
  294.0 2.2 fusion.32
  296.2 2.2 fusion.32
  298.5 1.4 copy-done.1
  300.0 2.9 multiply_reduce_fusion
  302.9 0.7 multiply_convert_fusion.2
  303.7 1.3 copy.67
  (78 shorter events, 11.2 us)
Async XLA Ops:
  9.6 77.0 %all-to-all-start.2 = ((bf16[2,2,2048]{2,1,0:T(2,128)(2,1)}), bf16[2,2,2048]{2,1,0:T(2,128)(2,1)S(1)}, u32[]{:S(2)}, u32[]{:S(2)}) async-start(bf16[2,2,2048]{2,1,0:T(2,128)(2,1)} %reshape.322), calls=%async_computation.2 | async-start | bytes 32768 | tf_op jit(solution)/shard_map/all_to_all | solution.py:72
  70.5 2.5 copy-start.3
  72.9 17.4 %copy-start.16 = (f32[64]{0:T(128)S(1)}, f32[64]{0:T(128)}, u32[]{:S(2)}) copy-start(f32[64]{0:T(128)} %param.20) | copy-start | bytes 772
  86.5 8.0 %all-to-all-start.1 = ((bf16[2,2,32768]{2,1,0:T(2,128)(2,1)}), bf16[2,2,32768]{2,1,0:T(2,128)(2,1)S(1)}, u32[]{:S(2)}, u32[]{:S(2)}) async-start(bf16[2,2,32768]{2,1,0:T(2,128)(2,1)} %reshape.324), calls=%async_computation.1 | async-start | bytes 524288 | tf_op jit(solution)/shard_map/all_to_all | solution.py:71
  91.6 10.0 %collective-permute-start.2 = (f32[4,1024]{1,0:T(4,128)S(1)}, f32[4,1024]{1,0:T(4,128)S(1)}, u32[]{:S(2)}, u32[]{:S(2)}) collective-permute-start(f32[4,1024]{1,0:T(4,128)S(1)} %broadcast_in_dim.63), channel_id=1, source_target_pairs={{0,1},{1,0},{2,3},{3,2},{4,5},{5,4},{6,7},{7,6},{8,9},{9,8},{10,11... | collective-permute-start | bytes 49160 | tf_op jit(solution)/shard_map/ppermute | solution.py:20
  94.5 15.7 %all-to-all-start = ((bf16[2,2,131072]{2,1,0:T(2,128)(2,1)}), bf16[2,2,131072]{2,1,0:T(2,128)(2,1)S(1)}, u32[]{:S(2)}, u32[]{:S(2)}) async-start(bf16[2,2,131072]{2,1,0:T(2,128)(2,1)} %reshape.320), calls=%async_computation | async-start | bytes 2097152 | tf_op jit(solution)/shard_map/all_to_all | solution.py:70
  98.1 191.4 %all-gather.5.cloned.1.call-start = ((), (), s32[]{:S(2)}) async-start(), calls=%async_computation.3 | async-start | bytes 10485760 | tf_op jit(solution)/shard_map/all_gather | solution.py:25
  100.3 4.1 %collective-permute-start.1 = (bf16[3,1024]{1,0:T(4,128)(2,1)S(1)}, bf16[3,1024]{1,0:T(4,128)(2,1)S(1)}, u32[]{:S(2)}, u32[]{:S(2)}) collective-permute-start(bf16[3,1024]{1,0:T(4,128)(2,1)S(1)} %slice.89), channel_id=1, source_target_pairs={{0,1},{1,4},{4,5},{5,8},{8,9},{9,12},{12,13},{2,3},{3,6},{6,7},{7,... | collective-permute-start | bytes 18440 | tf_op jit(solution)/shard_map/ppermute | solution.py:16
  121.1 2.7 copy-start.15
  122.5 5.1 %collective-permute-start = (bf16[3,4096]{1,0:T(4,128)(2,1)S(1)}, bf16[3,4096]{1,0:T(4,128)(2,1)S(1)}, u32[]{:S(2)}, u32[]{:S(2)}) collective-permute-start(bf16[3,4096]{1,0:T(4,128)(2,1)S(1)} %slice.84), channel_id=1, source_target_pairs={{0,1},{1,4},{4,5},{5,8},{8,9},{9,12},{12,13},{2,3},{3,6},{6,7},{7,... | collective-permute-start | bytes 73736 | tf_op jit(solution)/shard_map/ppermute | solution.py:16
  124.2 3.7 %copy-start.8 = (f32[1,4096]{1,0:T(1,128)S(1)}, f32[1,4096]{1,0:T(1,128)}, u32[]{:S(2)}) copy-start(f32[1,4096]{1,0:T(1,128)} %get-tuple-element.155) | copy-start | bytes 49156
  124.2 3.7 %copy-start.9 = (f32[1,4096]{1,0:T(1,128)S(1)}, f32[1,4096]{1,0:T(1,128)}, u32[]{:S(2)}) copy-start(f32[1,4096]{1,0:T(1,128)} %get-tuple-element.156) | copy-start | bytes 49156
  124.2 3.7 %copy-start.10 = (f32[1,4096]{1,0:T(1,128)S(1)}, f32[1,4096]{1,0:T(1,128)}, u32[]{:S(2)}) copy-start(f32[1,4096]{1,0:T(1,128)} %get-tuple-element.157) | copy-start | bytes 49156
  124.2 3.7 %copy-start.11 = (f32[1,4096]{1,0:T(1,128)S(1)}, f32[1,4096]{1,0:T(1,128)}, u32[]{:S(2)}) copy-start(f32[1,4096]{1,0:T(1,128)} %get-tuple-element.158) | copy-start | bytes 49156
  124.2 3.7 %copy-start.14 = (f32[4096]{0:T(1024)S(1)}, f32[4096]{0:T(1024)}, u32[]{:S(2)}) copy-start(f32[4096]{0:T(1024)} %param.17) | copy-start | bytes 49156
  129.8 1.4 copy-start
  130.8 0.7 copy-start.7
  132.2 6.5 %collective-permute-start.3 = (f32[4,1024,128]{2,1,0:T(8,128)S(1)}, f32[4,1024,128]{2,1,0:T(8,128)S(1)}, u32[]{:S(2)}, u32[]{:S(2)}) collective-permute-start(f32[4,1024,128]{2,1,0:T(8,128)S(1)} %convolution_add_fusion), channel_id=1, source_target_pairs={{0,1},{1,0},{2,3},{3,2},{4,5},{5,4},{6,7},{7,6},{8,9},{9,8},{10,11... | collective-permute-start | bytes 6291464 | tf_op jit(solution)/shard_map/ppermute | solution.py:20
  138.7 1.3 copy-start.2
  141.7 0.7 copy-start.17
  147.3 20.6 %copy-start.12 = (f32[1,128,64]{1,2,0:T(8,128)S(1)}, f32[1,128,64]{1,2,0:T(8,128)}, u32[]{:S(2)}) copy-start(f32[1,128,64]{1,2,0:T(8,128)} %get-tuple-element.150) | copy-start | bytes 98308
  147.3 20.6 %copy-start.13 = (f32[1,64,128]{2,1,0:T(8,128)S(1)}, f32[1,64,128]{2,1,0:T(8,128)}, u32[]{:S(2)}) copy-start(f32[1,64,128]{2,1,0:T(8,128)} %copy.62) | copy-start | bytes 98308
  289.6 8.8 %copy-start.4 = (f32[128,64]{0,1:T(8,128)S(1)}, f32[128,64]{0,1:T(8,128)}, u32[]{:S(2)}) copy-start(f32[128,64]{0,1:T(8,128)} %copy.65) | copy-start | bytes 98308
  298.4 1.6 copy-start.1
  298.4 1.6 copy-start.6
  300.0 3.0 copy-start.5
Sparse Core Ops, SparseCore 0:
  141.9 147.6 all-gather.4
where the time goes:
time: 317 us; the launch traced here: 312 us
  waiting for transfers between devices  135 us (43%)
  other arithmetic  74.1 us (23%)
  local copies, waits for them, and re-layouts  45.6 us (14%)
  blocking collectives  18.3 us (6%)
  starting transfers between devices  16.3 us (5%)
  between operations  13.9 us (4%)
  matrix products  8.53 us (3%)
    all_gather x1, waiting for transfers between devices, prefix_2(): everything = jax.tree.map(lambda part: lax.all_gather(part, axis), shard)  118 us
    unnamed x4, other arithmetic  57.9 us
    unnamed x46, local copies, waits for them, and re-layouts  22.8 us
    all_gather x1, blocking collectives, prefix_2(): everything = jax.tree.map(lambda part: lax.all_gather(part, axis), shard)  18.3 us
    all_to_all x3, local copies, waits for them, and re-layouts, on_device(): lax.all_to_all(x_raw, 'head', split_axis=2, concat_axis=1, tiled=True)  9.54 us
    select_n x4, other arithmetic, hop(): return jax.tree.map(lambda a, b: jnp.where(reached, a, b), new, before)  8.64 us
  transfers between devices with their start and end apart: 8, of which 6 were waited for; matrix products, arithmetic and copies ran while one was open for 29% of the time, Pallas kernels for 0%

commit v1 on v0

v1 whole, which is shorter than its diff:
```python
import functools
import jax
import jax.numpy as jnp
from jax import lax
from jax.experimental import pallas as pl
from jax.experimental.pallas import tpu as pltpu
from jax.sharding import PartitionSpec as P

STATE = 128
SPAN = 128
HEAD_DIM = 64
PER_GROUP = 16
WIDE = PER_GROUP * HEAD_DIM
PAIRS = PER_GROUP // 2
NORM_EPSILON = 1e-05
MESH = pl.DeviceIdType.MESH
F32 = jnp.float32
BF16 = jnp.bfloat16


def kernel(nseq, nhead, x_ref, bc_ref, dt_ref, wx_ref, bx_ref, wb_ref, bb_ref, par_ref, gain_ref, out_ref,
           xf, bcf, dtf, xc, bcc, ext, tail32, tail_out, tail_in, cum_sc, dt_sc, cumt_sc, dtt_sc, par_sc,
           end_out, end_in, st, sb, s0, ein, eout, cb, ysc, ecw,
           x_s, x_r, b_s, b_r, d_s, d_r, t_s, t_r, e_s, e_r, s_s, s_r, c_s, c_r, f_s, f_r):
    seq = lax.axis_index("seq")
    head = lax.axis_index("head")
    sub = lax.axis_index("sub")
    rows = x_ref.shape[1]
    groups = xf.shape[0]
    width = groups * WIDE
    bcw = groups * 2 * STATE
    heads = groups * PER_GROUP
    not_first = jnp.logical_or(seq > 0, sub > 0)
    not_last = jnp.logical_or(seq < nseq - 1, sub < 1)
    holds_tail = jnp.logical_and(not_last, head == nhead - 1)
    next_seq, prev_seq = seq + sub, seq + sub - 1
    other = 1 - sub
    lower, upper = sub == 0, sub == 1
    chain_in = jnp.logical_and(upper, seq > 0)
    chain_out = jnp.logical_and(upper, seq < nseq - 1)
    fwd_in = jnp.logical_and(lower, seq > 0)

    barrier = pltpu.get_barrier_semaphore()

    def tell(**where):
        pl.semaphore_signal(barrier, inc=1, device_id=where, device_id_type=MESH)

    partners = [lax.rem(head + d, nhead) for d in range(1, nhead)]
    for p in partners:
        tell(head=p)

    @pl.when(not_first)
    def _():
        tell(seq=prev_seq, sub=other, head=nhead - 1)

    @pl.when(upper)
    def _():
        tell(sub=0)

    @pl.when(fwd_in)
    def _():
        tell(sub=1)

    @pl.when(chain_in)
    def _():
        tell(seq=seq - 1)

    tail32[...] = jnp.zeros_like(tail32)
    for k in range(nhead):
        for j in range(groups):
            lo = k * width + j * WIDE
            tail32[3 * j:3 * j + 3, :] = x_ref[0, rows - 16:rows, lo:lo + WIDE].astype(F32)[13:16, :]
        lo = k * bcw
        tail32[12:15, 0:bcw] = bc_ref[0, rows - 16:rows, lo:lo + bcw].astype(F32)[13:16, :]
        tail_out[k] = tail32[...].astype(BF16)

    one = lambda cond: jnp.where(cond, 1, 0).astype(jnp.int32)
    peers = nhead - 1 + nhead * one(holds_tail) + one(lower) + one(chain_in) + one(chain_out)
    pl.semaphore_wait(barrier, peers)

    def remote(src, dst, send, recv, **where):
        return pltpu.make_async_remote_copy(
            src_ref=src, dst_ref=dst, send_sem=send, recv_sem=recv, device_id=where, device_id_type=MESH)

    mine = pl.ds(pl.multiple_of(head * rows, rows), rows)

    def x_copy(d, g):
        at = pl.ds(pl.multiple_of(partners[d] * width + g * WIDE, WIDE), WIDE)
        return remote(x_ref.at[0, :, at], xf.at[g, mine, :], x_s.at[d, g], x_r.at[d, g], head=partners[d])

    def bc_copy(d, g):
        at = pl.ds(pl.multiple_of(partners[d] * bcw + g * 2 * STATE, 2 * STATE), 2 * STATE)
        return remote(bc_ref.at[0, :, at], bcf.at[g, mine, :], b_s.at[d, g], b_r.at[d, g], head=partners[d])

    def dt_copy(d):
        return remote(dt_ref.at[0], dtf.at[mine, :], d_s.at[d], d_r.at[d], head=partners[d])

    def tail_copy(k):
        return remote(tail_out.at[k], tail_in, t_s.at[k], t_r, seq=next_seq, sub=other, head=k)

    def end_copy():
        return remote(end_out, end_in, e_s, e_r, sub=other)

    def s_copy(g):
        return remote(sb.at[g], s0.at[g], s_s.at[g], s_r.at[g], sub=other)

    def chain_copy(g):
        return remote(eout.at[g], ein.at[g], c_s.at[g], c_r.at[g], seq=seq + 1)

    def fwd_copy(g):
        return remote(ein.at[g], ein.at[g], f_s.at[g], f_r.at[g], sub=other)

    for d in range(nhead - 1):
        dt_copy(d).start()

    @pl.when(holds_tail)
    def _():
        for k in range(nhead):
            tail_copy(k).start()

    for g in range(groups):
        for d in range(nhead - 1):
            bc_copy(d, g).start()
            x_copy(d, g).start()

    for g in range(groups):
        at = pl.ds(pl.multiple_of(head * width + g * WIDE, WIDE), WIDE)
        xf[g, mine, :] = x_ref[0, :, at]
        at = pl.ds(pl.multiple_of(head * bcw + g * 2 * STATE, 2 * STATE), 2 * STATE)
        bcf[g, mine, :] = bc_ref[0, :, at]
    dtf[mine, :] = dt_ref[0]

    @pl.when(jnp.logical_not(not_first))
    def _():
        tail_in[...] = jnp.zeros_like(tail_in)

    @pl.when(seq == 0)
    def _():
        ein[...] = jnp.zeros_like(ein)

    for d in range(nhead - 1):
        dt_copy(d).wait_recv()
    dt_all = dtf[...].astype(F32)
    dt_own = dt_all
    for k in range(1, nhead):
        dt_own = jnp.where(head == k, pltpu.roll(dt_all, 128 - k * heads, 1), dt_own)
    par = par_ref[...]
    v = dt_own + par[0:1, :]
    u = jnp.exp(-jnp.abs(v))
    series = u * (1.0 - u * (0.5 - u * (1.0 / 3.0 - u * 0.25)))
    step = jnp.maximum(v, 0.0) + jnp.where(u < 0.03, series, jnp.log(1.0 + u))
    rate = -jnp.exp(par[1:2, :])
    row = lax.broadcasted_iota(jnp.int32, (SPAN, SPAN), 0)
    col = lax.broadcasted_iota(jnp.int32, (SPAN, SPAN), 1)
    causal = row >= col
    cum = jnp.dot(jnp.where(causal, 1.0, 0.0).astype(F32), rate * step,
                  preferred_element_type=F32, precision=lax.Precision.HIGHEST)
    cumt_sc[...] = jnp.transpose(cum)
    dtt_sc[...] = jnp.transpose(step)
    for g in range(groups):
        turn = (128 - g * PER_GROUP) % 128
        cum_g = pltpu.roll(cum, turn, 1) if turn else cum
        cum_sc[g] = cum_g
        dt_sc[g] = pltpu.roll(step, turn, 1) if turn else step
        par_sc[g] = pltpu.roll(par, turn, 1) if turn else par
        end_out[g] = jnp.broadcast_to(cum_g[SPAN - 1:SPAN, :], (8, 128))

    @pl.when(lower)
    def _():
        end_copy().start()

    @pl.when(upper)
    def _():
        end_copy().wait_recv()

    @pl.when(not_first)
    def _():
        tail_copy(0).wait_recv()

    tail32[...] = tail_in[...].astype(F32)
    left = col < HEAD_DIM

    def pair_wide(per_head, p):
        n = per_head.shape[0]
        a = jnp.broadcast_to(per_head[:, 2 * p:2 * p + 1], (n, 128))
        b = jnp.broadcast_to(per_head[:, 2 * p + 1:2 * p + 2], (n, 128))
        return jnp.where(left[0:n], a, b)

    def wide_row(per_head):
        return jnp.concatenate([pair_wide(per_head, p) for p in range(PAIRS)], axis=1)

    def conv(first, weights, bias, n):
        total = bias
        for k in range(4):
            total = total + weights[k:k + 1, :] * ext[5 + k:5 + k + SPAN, first:first + n]
        return (total * (1.0 / (1.0 + jnp.exp(-total)))).astype(BF16)

    for g in range(groups):
        for d in range(nhead - 1):
            bc_copy(d, g).wait_recv()
            x_copy(d, g).wait_recv()
        lo = g * WIDE
        blo = g * 2 * STATE
        ext[8:8 + SPAN, 0:WIDE] = xf[g].astype(F32)
        ext[8:8 + SPAN, WIDE:WIDE + 2 * STATE] = bcf[g].astype(F32)
        ext[5:8, 0:WIDE] = tail32[3 * g:3 * g + 3, :]
        ext[5:8, WIDE:WIDE + 2 * STATE] = tail32[12:15, blo:blo + 2 * STATE]
        bcc[g] = conv(WIDE, wb_ref[:, blo:blo + 2 * STATE], bb_ref[:, blo:blo + 2 * STATE], 2 * STATE)
        b_in = bcc[g, :, 0:STATE]
        for p in range(PAIRS):
            q = p * 128
            xcp = conv(q, wx_ref[:, lo + q:lo + q + 128], bx_ref[:, lo + q:lo + q + 128], 128)
            xc[g, :, q:q + 128] = xcp
            cum_p = pair_wide(cum_sc[g], p)
            ecw[g, :, q:q + 128] = jnp.exp(cum_p)
            to_end = jnp.exp(cum_p[SPAN - 1:SPAN, :] - cum_p) * pair_wide(dt_sc[g], p)
            cb[g, :, q:q + 128] = (to_end * xcp.astype(F32)).astype(BF16)
        state = lax.dot_general(b_in, cb[g], (((0,), (0,)), ((), ())), preferred_element_type=F32)

        @pl.when(lower)
        def _(state=state, g=g):
            sb[g] = state.astype(BF16)
            s_copy(g).start()

        @pl.when(upper)
        def _(state=state, g=g):
            st[g] = state

    def second(g, carry):
        @pl.when(upper)
        def _():
            @pl.when(chain_in)
            def _():
                chain_in_wait = remote(eout.at[g], ein.at[g], c_s.at[g], c_r.at[g], sub=other)
                chain_in_wait.wait_recv()
                fwd_copy(g).start()

            s_copy(g).wait_recv()
            d0 = jnp.exp(wide_row(end_in[g]))[0:1, :]
            d1 = jnp.exp(wide_row(end_out[g]))[0:1, :]
            carried = d0 * ein[g].astype(F32) + s0[g].astype(F32)
            cb[g] = carried.astype(BF16)

            @pl.when(chain_out)
            def _():
                eout[g] = (d1 * carried + st[g]).astype(BF16)
                chain_copy(g).start()

        inner = lax.dot_general(bcc[g, :, STATE:], bcc[g, :, 0:STATE], (((1,), (1,)), ((), ())),
                                preferred_element_type=F32)
        at = pl.ds(pl.multiple_of(g * PER_GROUP, PER_GROUP), PER_GROUP)
        cum_rows, dt_rows = cumt_sc[at, :], dtt_sc[at, :]
        cum_g = cum_sc[g]
        skip = par_sc[g]
        for p in range(PAIRS):
            mix = []
            for j in (2 * p, 2 * p + 1):
                gap = jnp.broadcast_to(cum_g[:, j:j + 1], (SPAN, SPAN)) - cum_rows[j:j + 1, :]
                w = jnp.exp(jnp.where(causal, gap, -1e30)) * dt_rows[j:j + 1, :]
                mix.append((inner * w).astype(BF16))
            xp = xc[g, :, p * 128:(p + 1) * 128]
            y = jnp.dot(jnp.concatenate(mix, axis=0), xp, preferred_element_type=F32)
            y = jnp.where(left, y[0:SPAN], y[SPAN:])
            ysc[g, :, p * 128:(p + 1) * 128] = y + pair_wide(skip, p)[2:3, :] * xp.astype(F32)
        return carry

    lax.fori_loop(0, groups, second, 0)

    def third(g, carry):
        @pl.when(lower)
        def _():
            @pl.when(fwd_in)
            def _():
                fwd_copy(g).wait_recv()

            cb[g] = ein[g]

        y = jnp.dot(bcc[g, :, STATE:], cb[g], preferred_element_type=F32)
        y = y * ecw[g] + ysc[g]
        mean = jnp.mean(y * y, axis=1, keepdims=True)
        at = pl.ds(pl.multiple_of(g * WIDE, WIDE), WIDE)
        out_ref[0, :, at] = (y * lax.rsqrt(mean + NORM_EPSILON) * gain_ref[:, at]).astype(BF16)
        return carry

    lax.fori_loop(0, groups, third, 0)

    for d in range(nhead - 1):
        dt_copy(d).wait_send()
        for g in range(groups):
            bc_copy(d, g).wait_send()
            x_copy(d, g).wait_send()

    @pl.when(holds_tail)
    def _():
        for k in range(nhead):
            tail_copy(k).wait_send()

    @pl.when(lower)
    def _():
        end_copy().wait_send()
        for g in range(groups):
            s_copy(g).wait_send()

    @pl.when(chain_in)
    def _():
        for g in range(groups):
            fwd_copy(g).wait_send()

    @pl.when(chain_out)
    def _():
        for g in range(groups):
            chain_copy(g).wait_send()


def on_device(nseq, nhead, x_raw, bc_raw, dt_raw, conv_x_weight, conv_x_bias, conv_bc_weight, conv_bc_bias,
              stride_offset_per_head, a_log, skip_d, norm_gain):
    width = conv_x_weight.shape[1]
    groups = width // WIDE
    heads = a_log.shape[0]
    par = jnp.pad(jnp.stack([stride_offset_per_head, a_log, skip_d]), ((0, 5), (0, 128 - heads)))
    V = pltpu.VMEM
    dma = lambda *s: pltpu.SemaphoreType.DMA(s)
    g3 = (groups, STATE, WIDE)
    return pl.pallas_call(
        functools.partial(kernel, nseq, nhead),
        out_shape=jax.ShapeDtypeStruct((1, SPAN, width), BF16),
        in_specs=[pl.BlockSpec(memory_space=pltpu.VMEM)] * 9,
        out_specs=pl.BlockSpec(memory_space=pltpu.VMEM),
        scratch_shapes=[
            V(g3, BF16), V((groups, SPAN, 2 * STATE), BF16), V((SPAN, 128), BF16),
            V(g3, BF16), V((groups, SPAN, 2 * STATE), BF16), V((SPAN + 8, WIDE + 2 * STATE), F32),
            V((16, WIDE), F32), V((nhead, 16, WIDE), BF16), V((16, WIDE), BF16),
            V((groups, SPAN, 128), F32), V((groups, SPAN, 128), F32), V((128, SPAN), F32), V((128, SPAN), F32),
            V((groups, 8, 128), F32), V((groups, 8, 128), F32), V((groups, 8, 128), F32),
            V(g3, F32), V(g3, BF16), V(g3, BF16), V(g3, BF16), V(g3, BF16), V(g3, BF16), V(g3, F32), V(g3, F32),
            dma(nhead - 1, groups), dma(nhead - 1, groups), dma(nhead - 1, groups), dma(nhead - 1, groups),
            dma(nhead - 1), dma(nhead - 1), dma(nhead), pltpu.SemaphoreType.DMA,
            pltpu.SemaphoreType.DMA, pltpu.SemaphoreType.DMA, dma(groups), dma(groups),
            dma(groups), dma(groups), dma(groups), dma(groups),
        ],
        compiler_params=pltpu.CompilerParams(
            collective_id=0, has_side_effects=True, vmem_limit_bytes=48 * 1024 * 1024),
    )(x_raw, bc_raw, dt_raw, conv_x_weight, conv_x_bias[None], conv_bc_weight, conv_bc_bias[None], par,
      norm_gain[None])


def solution(mesh):
    placed = (
        P(("groups", "seq", "sub"), "head", None),
        P(("groups", "seq", "sub"), "head", None),
        P(("groups", "seq", "sub"), "head", None),
        P(None, "head"),
        P("head"),
        P(None, "head"),
        P("head"),
        P("head"),
        P("head"),
        P("head"),
        P("head"),
    )
    return jax.shard_map(
        functools.partial(on_device, mesh.shape["seq"], mesh.shape["head"]),
        mesh=mesh,
        in_specs=placed,
        out_specs=P(("groups", "seq", "sub"), None, "head"),
        check_vma=False,
    )
```

time: 317 us -> 51.4 us (0.16); the launches traced: 312 us -> 50.9 us
  waiting for transfers between devices: 135 us -> 0 us
  other arithmetic: 74.1 us -> 0.71 us
  Pallas kernels: 0 us -> 43.3 us
  local copies, waits for them, and re-layouts: 45.6 us -> 6.82 us
  blocking collectives: 18.3 us -> 0 us
  starting transfers between devices: 16.3 us -> 0 us
  between operations: 13.9 us -> 0.03 us
  matrix products: 8.53 us -> 0 us
    all_gather x1 -> x0, waiting for transfers between devices: 118 us -> none  [prefix_2(): everything = jax.tree.map(lambda part: lax.all_gather(part, axis), shard)]
    unnamed x4 -> x0, other arithmetic: 57.9 us -> none
    pallas_call x0 -> x1, Pallas kernels: none -> 43.3 us  [on_device(): pl.pallas_call(functools.partial(kernel, nseq, nhead), out_shape=jax.Shap...]
    all_gather x1 -> x0, blocking collectives: 18.3 us -> none  [prefix_2(): everything = jax.tree.map(lambda part: lax.all_gather(part, axis), shard)]
    unnamed x46 -> x17, local copies, waits for them, and re-layouts: 22.8 us -> 6.82 us
    all_to_all x6 -> x0, local copies, waits for them, and re-layouts: 10.4 us -> none  [the longest x3 9.54 us: on_device(): lax.all_to_all(x_raw, 'head', split_axis=2, concat_axis=1, tiled=True)]
    all_to_all x3 -> x0, starting transfers between devices: 10.3 us -> none  [the longest x1 3.58 us: on_device(): lax.all_to_all(x_raw, 'head', split_axis=2, concat_axis=1, tiled=True)]
    select_n x5 -> x0, other arithmetic: 9.26 us -> none  [the longest x4 8.64 us: hop(): return jax.tree.map(lambda a, b: jnp.where(reached, a, b), new, before)]
  transfers between devices with their start and end apart: 8 -> 0, of which waited for: 6 -> 0; matrix products, arithmetic and copies ran while one was open for 29% -> 0% of each run, Pallas kernels for 0% -> 0%
where the time goes in v1:
time: 51.4 us; the launch traced here: 50.9 us
  Pallas kernels  43.3 us (84%)
  local copies, waits for them, and re-layouts  6.82 us (13%)
  other arithmetic  0.71 us (1%)
    pallas_call x1, Pallas kernels, on_device(): pl.pallas_call(functools.partial(kernel, nseq, nhead), out_shape=jax.Shap...  43.3 us
    unnamed x17, local copies, waits for them, and re-layouts  6.82 us

profile of v1, /device:TPU:29, one launch (start us, length us, event | category | flops | bytes accessed | tf_op | source)
XLA Modules:
  0.0 50.9 jit_solution(5101219010681789759)
XLA Ops:
  0.0 0.0 copy-start.3
  0.0 0.7 %select_maximum_fusion.par_ref = f32[8,128]{1,0:T(8,128)S(1)} fusion(f32[1,64]{1,0:T(1,128)} %bitcast.9, f32[1,64]{1,0:T(1,128)} %bitcast.10, f32[1,64]{1,0:T(1,128)} %bitcast.11), kind=kLoop, calls=%fused_computation | loop fusion | flops 11264 | bytes 4864 | tf_op jit(solution)/shard_map/stack | solution.py:320
  0.7 0.0 copy-done.3
  0.7 0.0 copy-start
  0.7 1.2 %copy-done = bf16[1,64,8192]{2,1,0:T(8,128)(2,1)S(1)} copy-done((bf16[1,64,8192]{2,1,0:T(8,128)(2,1)S(1)}, bf16[1,64,8192]{2,1,0:T(8,128)(2,1)}, u32[]{:S(2)}) %copy-start) | copy-done | bytes 1048600
  1.9 0.0 copy-start.1
  1.9 0.9 %copy-done.1 = bf16[1,64,2048]{2,1,0:T(8,128)(2,1)S(1)} copy-done((bf16[1,64,2048]{2,1,0:T(8,128)(2,1)S(1)}, bf16[1,64,2048]{2,1,0:T(8,128)(2,1)}, u32[]{:S(2)}) %copy-start.1) | copy-done | bytes 262168
  2.9 0.0 copy-start.2
  2.9 0.8 %copy-done.2 = f32[4,4096]{1,0:T(4,128)S(1)} copy-done((f32[4,4096]{1,0:T(4,128)S(1)}, f32[4,4096]{1,0:T(4,128)}, u32[]{:S(2)}) %copy-start.2) | copy-done | bytes 65560
  3.7 0.0 copy-start.4
  3.7 0.7 %copy-done.4 = f32[4096]{0:T(1024)S(1)} copy-done((f32[4096]{0:T(1024)S(1)}, f32[4096]{0:T(1024)}, u32[]{:S(2)}) %copy-start.4) | copy-done | bytes 16408
  4.5 0.0 copy-start.5
  4.5 0.7 %copy-done.5 = f32[4,1024]{1,0:T(4,128)S(1)} copy-done((f32[4,1024]{1,0:T(4,128)S(1)}, f32[4,1024]{1,0:T(4,128)}, u32[]{:S(2)}) %copy-start.5) | copy-done | bytes 16408
  5.2 0.0 copy-start.6
  5.2 0.7 %copy-done.6 = f32[4096]{0:T(1024)S(1)} copy-done((f32[4096]{0:T(1024)S(1)}, f32[4096]{0:T(1024)}, u32[]{:S(2)}) %copy-start.6) | copy-done | bytes 16408
  5.9 0.0 copy-start.7
  5.9 0.7 %copy-done.7 = f32[1024]{0:T(1024)S(1)} copy-done((f32[1024]{0:T(1024)S(1)}, f32[1024]{0:T(1024)}, u32[]{:S(2)}) %copy-start.7) | copy-done | bytes 4120
  6.6 43.3 %shard_map.109 = bf16[1,128,4096]{2,1,0:T(8,128)(2,1)S(1)} custom-call(bf16[1,64,8192]{2,1,0:T(8,128)(2,1)S(1)} %copy-done, bf16[1,64,2048]{2,1,0:T(8,128)(2,1)S(1)} %copy-done.1, bf16[1,64,128]{2,1,0:T(8,128)(2,1)S(1)} %copy-done.3, f32[4,4096]{1,0:T(4,128)S(1)} %copy-done.2, f32[1,4096]{1,0:T(1,128)S(1)} %bitcast.6, f32[4,1024]{1,0:T(4,128)S(1)} %copy-done.5, ...), custom_call_target="tpu_custom_call" | custom-call | tf_op jit(solution)/shard_map/pallas_call | solution.py:324
  49.9 1.0 %copy.13 = bf16[1,128,4096]{2,1,0:T(8,128)(2,1)} copy(bf16[1,128,4096]{2,1,0:T(8,128)(2,1)S(1)} %shard_map.109) | data formatting | bytes 2097152
Async XLA Ops:
  0.0 0.7 %copy-start.3 = (bf16[1,64,128]{2,1,0:T(8,128)(2,1)S(1)}, bf16[1,64,128]{2,1,0:T(8,128)(2,1)}, u32[]{:S(2)}) copy-start(bf16[1,64,128]{2,1,0:T(8,128)(2,1)} %dt_ref.1) | copy-start | bytes 49156
  0.7 1.2 %copy-start = (bf16[1,64,8192]{2,1,0:T(8,128)(2,1)S(1)}, bf16[1,64,8192]{2,1,0:T(8,128)(2,1)}, u32[]{:S(2)}) copy-start(bf16[1,64,8192]{2,1,0:T(8,128)(2,1)} %x_ref.1) | copy-start | bytes 3145732
  1.9 0.9 %copy-start.1 = (bf16[1,64,2048]{2,1,0:T(8,128)(2,1)S(1)}, bf16[1,64,2048]{2,1,0:T(8,128)(2,1)}, u32[]{:S(2)}) copy-start(bf16[1,64,2048]{2,1,0:T(8,128)(2,1)} %bc_ref.1) | copy-start | bytes 786436
  2.9 0.8 %copy-start.2 = (f32[4,4096]{1,0:T(4,128)S(1)}, f32[4,4096]{1,0:T(4,128)}, u32[]{:S(2)}) copy-start(f32[4,4096]{1,0:T(4,128)} %wx_ref.1) | copy-start | bytes 196612
  3.7 0.7 %copy-start.4 = (f32[4096]{0:T(1024)S(1)}, f32[4096]{0:T(1024)}, u32[]{:S(2)}) copy-start(f32[4096]{0:T(1024)} %param.15) | copy-start | bytes 49156
  4.5 0.7 %copy-start.5 = (f32[4,1024]{1,0:T(4,128)S(1)}, f32[4,1024]{1,0:T(4,128)}, u32[]{:S(2)}) copy-start(f32[4,1024]{1,0:T(4,128)} %wb_ref.1) | copy-start | bytes 49156
  5.2 0.7 %copy-start.6 = (f32[4096]{0:T(1024)S(1)}, f32[4096]{0:T(1024)}, u32[]{:S(2)}) copy-start(f32[4096]{0:T(1024)} %param.21) | copy-start | bytes 49156
  5.9 0.7 %copy-start.7 = (f32[1024]{0:T(1024)S(1)}, f32[1024]{0:T(1024)}, u32[]{:S(2)}) copy-start(f32[1024]{0:T(1024)} %param.17) | copy-start | bytes 12292

commit v2 on v1

--- a/solution.py
+++ b/solution.py
@@ -18,7 +18,8 @@
 BF16 = jnp.bfloat16
 
 
-def kernel(nseq, nhead, x_ref, bc_ref, dt_ref, wx_ref, bx_ref, wb_ref, bb_ref, par_ref, gain_ref, out_ref,
+def kernel(nseq, nhead, x_ref, bc_ref, dt_ref, wx_hbm, bx_hbm, wb_hbm, bb_hbm, par_hbm, gain_hbm, out_ref,
+           wx_ref, bx_ref, wb_ref, bb_ref, par_ref, gain_ref, x_last, bc_last, par_l, x_l, b_l,
            xf, bcf, dtf, xc, bcc, ext, tail32, tail_out, tail_in, cum_sc, dt_sc, cumt_sc, dtt_sc, par_sc,
            end_out, end_in, st, sb, s0, ein, eout, cb, ysc, ecw,
            x_s, x_r, b_s, b_r, d_s, d_r, t_s, t_r, e_s, e_r, s_s, s_r, c_s, c_r, f_s, f_r):
@@ -65,13 +66,31 @@
     def _():
         tell(seq=seq - 1)
 
+    local = []
+    for src, dst in ((x_ref.at[0, pl.ds(rows - 16, 16), :], x_last), (bc_ref.at[0, pl.ds(rows - 16, 16), :], bc_last),
+                     (par_hbm, par_ref), (wx_hbm, wx_ref), (bx_hbm, bx_ref), (wb_hbm, wb_ref), (bb_hbm, bb_ref),
+                     (gain_hbm, gain_ref)):
+        local.append(pltpu.make_async_copy(src, dst, par_l.at[len(local)]))
+    mine = pl.ds(pl.multiple_of(head * rows, rows), rows)
+    local.append(pltpu.make_async_copy(dt_ref.at[0], dtf.at[mine, :], par_l.at[len(local)]))
+    own = []
+    for g in range(groups):
+        at = pl.ds(pl.multiple_of(head * width + g * WIDE, WIDE), WIDE)
+        bat = pl.ds(pl.multiple_of(head * bcw + g * 2 * STATE, 2 * STATE), 2 * STATE)
+        own.append((pltpu.make_async_copy(x_ref.at[0, :, at], xf.at[g, mine, :], x_l.at[g]),
+                    pltpu.make_async_copy(bc_ref.at[0, :, bat], bcf.at[g, mine, :], b_l.at[g])))
+    for copy in local:
+        copy.start()
+
+    local[0].wait()
+    local[1].wait()
     tail32[...] = jnp.zeros_like(tail32)
     for k in range(nhead):
         for j in range(groups):
             lo = k * width + j * WIDE
-            tail32[3 * j:3 * j + 3, :] = x_ref[0, rows - 16:rows, lo:lo + WIDE].astype(F32)[13:16, :]
+            tail32[3 * j:3 * j + 3, :] = x_last[:, lo:lo + WIDE].astype(F32)[13:16, :]
         lo = k * bcw
-        tail32[12:15, 0:bcw] = bc_ref[0, rows - 16:rows, lo:lo + bcw].astype(F32)[13:16, :]
+        tail32[12:15, 0:bcw] = bc_last[:, lo:lo + bcw].astype(F32)[13:16, :]
         tail_out[k] = tail32[...].astype(BF16)
 
     one = lambda cond: jnp.where(cond, 1, 0).astype(jnp.int32)
@@ -81,8 +100,6 @@
     def remote(src, dst, send, recv, **where):
         return pltpu.make_async_remote_copy(
             src_ref=src, dst_ref=dst, send_sem=send, recv_sem=recv, device_id=where, device_id_type=MESH)
-
-    mine = pl.ds(pl.multiple_of(head * rows, rows), rows)
 
     def x_copy(d, g):
         at = pl.ds(pl.multiple_of(partners[d] * width + g * WIDE, WIDE), WIDE)
@@ -123,12 +140,9 @@
             bc_copy(d, g).start()
             x_copy(d, g).start()
 
-    for g in range(groups):
-        at = pl.ds(pl.multiple_of(head * width + g * WIDE, WIDE), WIDE)
-        xf[g, mine, :] = x_ref[0, :, at]
-        at = pl.ds(pl.multiple_of(head * bcw + g * 2 * STATE, 2 * STATE), 2 * STATE)
-        bcf[g, mine, :] = bc_ref[0, :, at]
-    dtf[mine, :] = dt_ref[0]
+    for x_own, bc_own in own:
+        bc_own.start()
+        x_own.start()
 
     @pl.when(jnp.logical_not(not_first))
     def _():
@@ -140,6 +154,8 @@
 
     for d in range(nhead - 1):
         dt_copy(d).wait_recv()
+    for copy in local[2:]:
+        copy.wait()
     dt_all = dtf[...].astype(F32)
     dt_own = dt_all
     for k in range(1, nhead):
@@ -195,7 +211,32 @@
             total = total + weights[k:k + 1, :] * ext[5 + k:5 + k + SPAN, first:first + n]
         return (total * (1.0 / (1.0 + jnp.exp(-total)))).astype(BF16)
 
+    lag = jnp.minimum(1 + 2 * seq, 2 * groups)
+
+    def chain(slot):
+        g = slot - lag
+
+        @pl.when(jnp.logical_and(upper, jnp.logical_and(g >= 0, g < groups)))
+        def _():
+            @pl.when(chain_in)
+            def _():
+                remote(eout.at[g], ein.at[g], c_s.at[g], c_r.at[g], sub=other).wait_recv()
+                fwd_copy(g).start()
+
+            s_copy(g).wait_recv()
+            d0 = jnp.exp(wide_row(end_in[g]))[0:1, :]
+            d1 = jnp.exp(wide_row(end_out[g]))[0:1, :]
+            carried = d0 * ein[g].astype(F32) + s0[g].astype(F32)
+            cb[g] = carried.astype(BF16)
+
+            @pl.when(chain_out)
+            def _():
+                eout[g] = (d1 * carried + st[g]).astype(BF16)
+                chain_copy(g).start()
+
     for g in range(groups):
+        own[g][0].wait()
+        own[g][1].wait()
         for d in range(nhead - 1):
             bc_copy(d, g).wait_recv()
             x_copy(d, g).wait_recv()
@@ -226,26 +267,9 @@
         def _(state=state, g=g):
             st[g] = state
 
+        chain(g)
+
     def second(g, carry):
-        @pl.when(upper)
-        def _():
-            @pl.when(chain_in)
-            def _():
-                chain_in_wait = remote(eout.at[g], ein.at[g], c_s.at[g], c_r.at[g], sub=other)
-                chain_in_wait.wait_recv()
-                fwd_copy(g).start()
-
-            s_copy(g).wait_recv()
-            d0 = jnp.exp(wide_row(end_in[g]))[0:1, :]
-            d1 = jnp.exp(wide_row(end_out[g]))[0:1, :]
-            carried = d0 * ein[g].astype(F32) + s0[g].astype(F32)
-            cb[g] = carried.astype(BF16)
-
-            @pl.when(chain_out)
-            def _():
-                eout[g] = (d1 * carried + st[g]).astype(BF16)
-                chain_copy(g).start()
-
         inner = lax.dot_general(bcc[g, :, STATE:], bcc[g, :, 0:STATE], (((1,), (1,)), ((), ())),
                                 preferred_element_type=F32)
         at = pl.ds(pl.multiple_of(g * PER_GROUP, PER_GROUP), PER_GROUP)
@@ -262,11 +286,14 @@
             y = jnp.dot(jnp.concatenate(mix, axis=0), xp, preferred_element_type=F32)
             y = jnp.where(left, y[0:SPAN], y[SPAN:])
             ysc[g, :, p * 128:(p + 1) * 128] = y + pair_wide(skip, p)[2:3, :] * xp.astype(F32)
+        chain(groups + g)
         return carry
 
     lax.fori_loop(0, groups, second, 0)
 
     def third(g, carry):
+        chain(2 * groups + g)
+
         @pl.when(lower)
         def _():
             @pl.when(fwd_in)
@@ -324,9 +351,12 @@
     return pl.pallas_call(
         functools.partial(kernel, nseq, nhead),
         out_shape=jax.ShapeDtypeStruct((1, SPAN, width), BF16),
-        in_specs=[pl.BlockSpec(memory_space=pltpu.VMEM)] * 9,
+        in_specs=[pl.BlockSpec(memory_space=pltpu.HBM)] * 9,
         out_specs=pl.BlockSpec(memory_space=pltpu.VMEM),
         scratch_shapes=[
+            V(conv_x_weight.shape, F32), V((1, width), F32), V(conv_bc_weight.shape, F32),
+            V((1, conv_bc_weight.shape[1]), F32), V((8, 128), F32), V((1, width), F32),
+            V((16, x_raw.shape[2]), BF16), V((16, bc_raw.shape[2]), BF16), dma(9), dma(groups), dma(groups),
             V(g3, BF16), V((groups, SPAN, 2 * STATE), BF16), V((SPAN, 128), BF16),
             V(g3, BF16), V((groups, SPAN, 2 * STATE), BF16), V((SPAN + 8, WIDE + 2 * STATE), F32),
             V((16, WIDE), F32), V((nhead, 16, WIDE), BF16), V((16, WIDE), BF16),
@@ -339,7 +369,7 @@
             dma(groups), dma(groups), dma(groups), dma(groups),
         ],
         compiler_params=pltpu.CompilerParams(
-            collective_id=0, has_side_effects=True, vmem_limit_bytes=48 * 1024 * 1024),
+            collective_id=0, has_side_effects=True, vmem_limit_bytes=64 * 1024 * 1024 - 131072),
     )(x_raw, bc_raw, dt_raw, conv_x_weight, conv_x_bias[None], conv_bc_weight, conv_bc_bias[None], par,
       norm_gain[None])
 

time: 51.4 us -> 43.5 us (0.85)
  local copies, waits for them, and re-layouts: 6.82 us -> 2.97 us
  Pallas kernels: 43.3 us -> 39.7 us
    unnamed x17 -> x7, local copies, waits for them, and re-layouts: 6.82 us -> 2.97 us
    pallas_call x1, Pallas kernels: 43.3 us -> 39.7 us  [on_device(): pl.pallas_call(functools.partial(kernel, nseq, nhead), out_shape=jax.Shap...]
where the time goes in v2:
time: 43.5 us; the launch traced here: 43.3 us
  Pallas kernels  39.7 us (91%)
  local copies, waits for them, and re-layouts  2.97 us (7%)
  other arithmetic  0.6 us (1%)
    pallas_call x1, Pallas kernels, on_device(): pl.pallas_call(functools.partial(kernel, nseq, nhead), out_shape=jax.Shap...  39.7 us
    unnamed x7, local copies, waits for them, and re-layouts  2.97 us

profile of v2, /device:TPU:29, one launch (start us, length us, event | category | flops | bytes accessed | tf_op | source)
XLA Modules:
  0.0 43.3 jit_solution(13018155593920226367)
XLA Ops:
  0.0 0.0 copy-start
  0.0 0.0 copy-start.1
  0.0 0.0 copy-start.2
  0.0 0.6 %copy-done = f32[64]{0:T(128)S(1)} copy-done((f32[64]{0:T(128)S(1)}, f32[64]{0:T(128)}, u32[]{:S(2)}) %copy-start) | copy-done | bytes 280
  0.7 0.0 copy-done.1
  0.7 0.0 copy-done.2
  0.7 0.6 %select_maximum_fusion.par_hbm = f32[8,128]{1,0:T(8,128)} fusion(f32[1,64]{1,0:T(1,128)S(1)} %bitcast.9, f32[1,64]{1,0:T(1,128)S(1)} %bitcast.10, f32[1,64]{1,0:T(1,128)S(1)} %bitcast.11), kind=kLoop, calls=%fused_computation | loop fusion | flops 11264 | bytes 4864 | tf_op jit(solution)/shard_map/stack | solution.py:347
  1.3 39.7 %shard_map.109 = bf16[1,128,4096]{2,1,0:T(8,128)(2,1)} custom-call(bf16[1,64,8192]{2,1,0:T(8,128)(2,1)} %x_ref.1, bf16[1,64,2048]{2,1,0:T(8,128)(2,1)} %bc_ref.1, bf16[1,64,128]{2,1,0:T(8,128)(2,1)} %dt_ref.1, f32[4,4096]{1,0:T(4,128)} %wx_hbm.1, f32[1,4096]{1,0:T(1,128)} %bitcast.6, f32[4,1024]{1,0:T(4,128)} %wb_hbm.1, f32[1,1024]{1,0:T(1,128)} %bitcast.8, ...), custom_call_target="tpu_custom_call" | custom-call | tf_op jit(solution)/shard_map/pallas_call | solution.py:351
  41.0 2.3 %copy.13 = bf16[1,128,4096]{2,1,0:T(8,128)(2,1)} copy(bf16[1,128,4096]{2,1,0:T(8,128)(2,1)} %shard_map.109) | data formatting | bytes 2097152
Async XLA Ops:
  0.0 0.7 %copy-start = (f32[64]{0:T(128)S(1)}, f32[64]{0:T(128)}, u32[]{:S(2)}) copy-start(f32[64]{0:T(128)} %param.20) | copy-start | bytes 772
  0.0 0.7 %copy-start.1 = (f32[64]{0:T(128)S(1)}, f32[64]{0:T(128)}, u32[]{:S(2)}) copy-start(f32[64]{0:T(128)} %param.19) | copy-start | bytes 772
  0.0 0.7 %copy-start.2 = (f32[64]{0:T(128)S(1)}, f32[64]{0:T(128)}, u32[]{:S(2)}) copy-start(f32[64]{0:T(128)} %param.18) | copy-start | bytes 772

commit v3 on v2

--- a/solution.py
+++ b/solution.py
@@ -13,6 +13,8 @@
 WIDE = PER_GROUP * HEAD_DIM
 PAIRS = PER_GROUP // 2
 NORM_EPSILON = 1e-05
+PARTS = 4
+PART = STATE // PARTS
 MESH = pl.DeviceIdType.MESH
 F32 = jnp.float32
 BF16 = jnp.bfloat16
@@ -82,6 +84,47 @@
     for copy in local:
         copy.start()
 
+    one = lambda cond: jnp.where(cond, 1, 0).astype(jnp.int32)
+    peers = nhead - 1 + nhead * one(holds_tail) + one(lower) + one(chain_in) + one(chain_out)
+    pl.semaphore_wait(barrier, peers)
+
+    def remote(src, dst, send, recv, **where):
+        return pltpu.make_async_remote_copy(
+            src_ref=src, dst_ref=dst, send_sem=send, recv_sem=recv, device_id=where, device_id_type=MESH)
+
+    def x_copy(d, g):
+        at = pl.ds(pl.multiple_of(partners[d] * width + g * WIDE, WIDE), WIDE)
+        return remote(x_ref.at[0, :, at], xf.at[g, mine, :], x_s.at[d, g], x_r.at[d, g], head=partners[d])
+
+    def bc_copy(d, g):
+        at = pl.ds(pl.multiple_of(partners[d] * bcw + g * 2 * STATE, 2 * STATE), 2 * STATE)
+        return remote(bc_ref.at[0, :, at], bcf.at[g, mine, :], b_s.at[d, g], b_r.at[d, g], head=partners[d])
+
+    def dt_copy(d):
+        return remote(dt_ref.at[0], dtf.at[mine, :], d_s.at[d], d_r.at[d], head=partners[d])
+
+    def tail_copy(k):
+        return remote(tail_out.at[k], tail_in, t_s.at[k], t_r, seq=next_seq, sub=other, head=k)
+
+    def end_copy():
+        return remote(end_out, end_in, e_s, e_r, sub=other)
+
+    def s_copy(g):
+        return remote(sb.at[g], s0.at[g], s_s.at[g], s_r.at[g], sub=other)
+
+    def chain_copy(g, i):
+        at = pl.ds(i * PART, PART)
+        return remote(eout.at[g, at], ein.at[g, at], c_s.at[g, i], c_r.at[g, i], seq=seq + 1)
+
+    def fwd_copy(g, i):
+        at = pl.ds(i * PART, PART)
+        return remote(ein.at[g, at], ein.at[g, at], f_s.at[g, i], f_r.at[g, i], sub=other)
+
+    for d in range(nhead - 1):
+        dt_copy(d).start()
+        bc_copy(d, 0).start()
+        x_copy(d, 0).start()
+
     local[0].wait()
     local[1].wait()
     tail32[...] = jnp.zeros_like(tail32)
@@ -93,49 +136,12 @@
         tail32[12:15, 0:bcw] = bc_last[:, lo:lo + bcw].astype(F32)[13:16, :]
         tail_out[k] = tail32[...].astype(BF16)
 
-    one = lambda cond: jnp.where(cond, 1, 0).astype(jnp.int32)
-    peers = nhead - 1 + nhead * one(holds_tail) + one(lower) + one(chain_in) + one(chain_out)
-    pl.semaphore_wait(barrier, peers)
-
-    def remote(src, dst, send, recv, **where):
-        return pltpu.make_async_remote_copy(
-            src_ref=src, dst_ref=dst, send_sem=send, recv_sem=recv, device_id=where, device_id_type=MESH)
-
-    def x_copy(d, g):
-        at = pl.ds(pl.multiple_of(partners[d] * width + g * WIDE, WIDE), WIDE)
-        return remote(x_ref.at[0, :, at], xf.at[g, mine, :], x_s.at[d, g], x_r.at[d, g], head=partners[d])
-
-    def bc_copy(d, g):
-        at = pl.ds(pl.multiple_of(partners[d] * bcw + g * 2 * STATE, 2 * STATE), 2 * STATE)
-        return remote(bc_ref.at[0, :, at], bcf.at[g, mine, :], b_s.at[d, g], b_r.at[d, g], head=partners[d])
-
-    def dt_copy(d):
-        return remote(dt_ref.at[0], dtf.at[mine, :], d_s.at[d], d_r.at[d], head=partners[d])
-
-    def tail_copy(k):
-        return remote(tail_out.at[k], tail_in, t_s.at[k], t_r, seq=next_seq, sub=other, head=k)
-
-    def end_copy():
-        return remote(end_out, end_in, e_s, e_r, sub=other)
-
-    def s_copy(g):
-        return remote(sb.at[g], s0.at[g], s_s.at[g], s_r.at[g], sub=other)
-
-    def chain_copy(g):
-        return remote(eout.at[g], ein.at[g], c_s.at[g], c_r.at[g], seq=seq + 1)
-
-    def fwd_copy(g):
-        return remote(ein.at[g], ein.at[g], f_s.at[g], f_r.at[g], sub=other)
-
-    for d in range(nhead - 1):
-        dt_copy(d).start()
-
     @pl.when(holds_tail)
     def _():
         for k in range(nhead):
             tail_copy(k).start()
 
-    for g in range(groups):
+    for g in range(1, groups):
         for d in range(nhead - 1):
             bc_copy(d, g).start()
             x_copy(d, g).start()
@@ -218,21 +224,24 @@
 
         @pl.when(jnp.logical_and(upper, jnp.logical_and(g >= 0, g < groups)))
         def _():
-            @pl.when(chain_in)
-            def _():
-                remote(eout.at[g], ein.at[g], c_s.at[g], c_r.at[g], sub=other).wait_recv()
-                fwd_copy(g).start()
-
             s_copy(g).wait_recv()
             d0 = jnp.exp(wide_row(end_in[g]))[0:1, :]
             d1 = jnp.exp(wide_row(end_out[g]))[0:1, :]
-            carried = d0 * ein[g].astype(F32) + s0[g].astype(F32)
-            cb[g] = carried.astype(BF16)
-
-            @pl.when(chain_out)
-            def _():
-                eout[g] = (d1 * carried + st[g]).astype(BF16)
-                chain_copy(g).start()
+            for i in range(PARTS):
+                at = slice(i * PART, (i + 1) * PART)
+
+                @pl.when(chain_in)
+                def _(i=i):
+                    chain_copy(g, i).wait_recv()
+                    fwd_copy(g, i).start()
+
+                carried = d0 * ein[g, at, :].astype(F32) + s0[g, at, :].astype(F32)
+                cb[g, at, :] = carried.astype(BF16)
+
+                @pl.when(chain_out)
+                def _(i=i, at=at, carried=carried):
+                    eout[g, at, :] = (d1 * carried + st[g, at, :]).astype(BF16)
+                    chain_copy(g, i).start()
 
     for g in range(groups):
         own[g][0].wait()
@@ -298,7 +307,8 @@
         def _():
             @pl.when(fwd_in)
             def _():
-                fwd_copy(g).wait_recv()
+                for i in range(PARTS):
+                    fwd_copy(g, i).wait_recv()
 
             cb[g] = ein[g]
 
@@ -331,12 +341,14 @@
     @pl.when(chain_in)
     def _():
         for g in range(groups):
-            fwd_copy(g).wait_send()
+            for i in range(PARTS):
+                fwd_copy(g, i).wait_send()
 
     @pl.when(chain_out)
     def _():
         for g in range(groups):
-            chain_copy(g).wait_send()
+            for i in range(PARTS):
+                chain_copy(g, i).wait_send()
 
 
 def on_device(nseq, nhead, x_raw, bc_raw, dt_raw, conv_x_weight, conv_x_bias, conv_bc_weight, conv_bc_bias,
@@ -366,7 +378,7 @@
             dma(nhead - 1, groups), dma(nhead - 1, groups), dma(nhead - 1, groups), dma(nhead - 1, groups),
             dma(nhead - 1), dma(nhead - 1), dma(nhead), pltpu.SemaphoreType.DMA,
             pltpu.SemaphoreType.DMA, pltpu.SemaphoreType.DMA, dma(groups), dma(groups),
-            dma(groups), dma(groups), dma(groups), dma(groups),
+            dma(groups, PARTS), dma(groups, PARTS), dma(groups, PARTS), dma(groups, PARTS),
         ],
         compiler_params=pltpu.CompilerParams(
             collective_id=0, has_side_effects=True, vmem_limit_bytes=64 * 1024 * 1024 - 131072),

time: 43.5 us -> 41.5 us (0.954)
  Pallas kernels: 39.7 us -> 37.6 us
    pallas_call x1, Pallas kernels: 39.7 us -> 37.6 us  [on_device(): pl.pallas_call(functools.partial(kernel, nseq, nhead), out_shape=jax.Shap...]
where the time goes in v3:
time: 41.5 us; the launch traced here: 41.2 us
  Pallas kernels  37.6 us (91%)
  local copies, waits for them, and re-layouts  2.97 us (7%)
  other arithmetic  0.6 us (1%)
    pallas_call x1, Pallas kernels, on_device(): pl.pallas_call(functools.partial(kernel, nseq, nhead), out_shape=jax.Shap...  37.6 us
    unnamed x7, local copies, waits for them, and re-layouts  2.97 us

profile of v3, /device:TPU:29, one launch (start us, length us, event | category | flops | bytes accessed | tf_op | source)
XLA Modules:
  0.0 41.2 jit_solution(15230520361483033366)
XLA Ops:
  0.0 0.0 copy-start
  0.0 0.0 copy-start.1
  0.0 0.0 copy-start.2
  0.0 0.6 %copy-done = f32[64]{0:T(128)S(1)} copy-done((f32[64]{0:T(128)S(1)}, f32[64]{0:T(128)}, u32[]{:S(2)}) %copy-start) | copy-done | bytes 280
  0.7 0.0 copy-done.1
  0.7 0.0 copy-done.2
  0.7 0.6 %select_maximum_fusion.par_hbm = f32[8,128]{1,0:T(8,128)} fusion(f32[1,64]{1,0:T(1,128)S(1)} %bitcast.9, f32[1,64]{1,0:T(1,128)S(1)} %bitcast.10, f32[1,64]{1,0:T(1,128)S(1)} %bitcast.11), kind=kLoop, calls=%fused_computation | loop fusion | flops 11264 | bytes 4864 | tf_op jit(solution)/shard_map/stack | solution.py:359
  1.3 37.6 %shard_map.109 = bf16[1,128,4096]{2,1,0:T(8,128)(2,1)} custom-call(bf16[1,64,8192]{2,1,0:T(8,128)(2,1)} %x_ref.1, bf16[1,64,2048]{2,1,0:T(8,128)(2,1)} %bc_ref.1, bf16[1,64,128]{2,1,0:T(8,128)(2,1)} %dt_ref.1, f32[4,4096]{1,0:T(4,128)} %wx_hbm.1, f32[1,4096]{1,0:T(1,128)} %bitcast.6, f32[4,1024]{1,0:T(4,128)} %wb_hbm.1, f32[1,1024]{1,0:T(1,128)} %bitcast.8, ...), custom_call_target="tpu_custom_call" | custom-call | tf_op jit(solution)/shard_map/pallas_call | solution.py:363
  38.9 2.3 %copy.13 = bf16[1,128,4096]{2,1,0:T(8,128)(2,1)} copy(bf16[1,128,4096]{2,1,0:T(8,128)(2,1)} %shard_map.109) | data formatting | bytes 2097152
Async XLA Ops:
  0.0 0.7 %copy-start = (f32[64]{0:T(128)S(1)}, f32[64]{0:T(128)}, u32[]{:S(2)}) copy-start(f32[64]{0:T(128)} %param.20) | copy-start | bytes 772
  0.0 0.7 %copy-start.1 = (f32[64]{0:T(128)S(1)}, f32[64]{0:T(128)}, u32[]{:S(2)}) copy-start(f32[64]{0:T(128)} %param.19) | copy-start | bytes 772
  0.0 0.7 %copy-start.2 = (f32[64]{0:T(128)S(1)}, f32[64]{0:T(128)}, u32[]{:S(2)}) copy-start(f32[64]{0:T(128)} %param.18) | copy-start | bytes 772

commit v4 on v3

--- a/solution.py
+++ b/solution.py
@@ -217,7 +217,7 @@
             total = total + weights[k:k + 1, :] * ext[5 + k:5 + k + SPAN, first:first + n]
         return (total * (1.0 / (1.0 + jnp.exp(-total)))).astype(BF16)
 
-    lag = jnp.minimum(1 + 2 * seq, 2 * groups)
+    lag = jnp.minimum(2 * seq + one(seq == 0), groups + 2)
 
     def chain(slot):
         g = slot - lag
@@ -242,6 +242,24 @@
                 def _(i=i, at=at, carried=carried):
                     eout[g, at, :] = (d1 * carried + st[g, at, :]).astype(BF16)
                     chain_copy(g, i).start()
+
+    def within(g):
+        inner = lax.dot_general(bcc[g, :, STATE:], bcc[g, :, 0:STATE], (((1,), (1,)), ((), ())),
+                                preferred_element_type=F32)
+        at = slice(g * PER_GROUP, (g + 1) * PER_GROUP)
+        cum_rows, dt_rows = cumt_sc[at, :], dtt_sc[at, :]
+        cum_g = cum_sc[g]
+        skip = par_sc[g]
+        for p in range(PAIRS):
+            mix = []
+            for j in (2 * p, 2 * p + 1):
+                gap = jnp.broadcast_to(cum_g[:, j:j + 1], (SPAN, SPAN)) - cum_rows[j:j + 1, :]
+                w = jnp.exp(jnp.where(causal, gap, -1e30)) * dt_rows[j:j + 1, :]
+                mix.append((inner * w).astype(BF16))
+            xp = xc[g, :, p * 128:(p + 1) * 128]
+            y = jnp.dot(jnp.concatenate(mix, axis=0), xp, preferred_element_type=F32)
+            y = jnp.where(left, y[0:SPAN], y[SPAN:])
+            ysc[g, :, p * 128:(p + 1) * 128] = y + pair_wide(skip, p)[2:3, :] * xp.astype(F32)
 
     for g in range(groups):
         own[g][0].wait()
@@ -277,31 +295,15 @@
             st[g] = state
 
         chain(g)
-
-    def second(g, carry):
-        inner = lax.dot_general(bcc[g, :, STATE:], bcc[g, :, 0:STATE], (((1,), (1,)), ((), ())),
-                                preferred_element_type=F32)
-        at = pl.ds(pl.multiple_of(g * PER_GROUP, PER_GROUP), PER_GROUP)
-        cum_rows, dt_rows = cumt_sc[at, :], dtt_sc[at, :]
-        cum_g = cum_sc[g]
-        skip = par_sc[g]
-        for p in range(PAIRS):
-            mix = []
-            for j in (2 * p, 2 * p + 1):
-                gap = jnp.broadcast_to(cum_g[:, j:j + 1], (SPAN, SPAN)) - cum_rows[j:j + 1, :]
-                w = jnp.exp(jnp.where(causal, gap, -1e30)) * dt_rows[j:j + 1, :]
-                mix.append((inner * w).astype(BF16))
-            xp = xc[g, :, p * 128:(p + 1) * 128]
-            y = jnp.dot(jnp.concatenate(mix, axis=0), xp, preferred_element_type=F32)
-            y = jnp.where(left, y[0:SPAN], y[SPAN:])
-            ysc[g, :, p * 128:(p + 1) * 128] = y + pair_wide(skip, p)[2:3, :] * xp.astype(F32)
-        chain(groups + g)
-        return carry
-
-    lax.fori_loop(0, groups, second, 0)
+        if g > 0:
+            within(g - 1)
+
+    chain(groups)
+    within(groups - 1)
+    chain(groups + 1)
 
     def third(g, carry):
-        chain(2 * groups + g)
+        chain(groups + 2 + g)
 
         @pl.when(lower)
         def _():

time: 41.5 us -> 40.1 us (0.966)
  Pallas kernels: 37.6 us -> 36.3 us
    pallas_call x1, Pallas kernels: 37.6 us -> 36.3 us  [on_device(): pl.pallas_call(functools.partial(kernel, nseq, nhead), out_shape=jax.Shap...]
where the time goes in v4:
time: 40.1 us; the launch traced here: 39.9 us
  Pallas kernels  36.3 us (91%)
  local copies, waits for them, and re-layouts  2.97 us (7%)
  other arithmetic  0.6 us (1%)
    pallas_call x1, Pallas kernels, on_device(): pl.pallas_call(functools.partial(kernel, nseq, nhead), out_shape=jax.Shap...  36.3 us
    unnamed x7, local copies, waits for them, and re-layouts  2.97 us

profile of v4, /device:TPU:29, one launch (start us, length us, event | category | flops | bytes accessed | tf_op | source)
XLA Modules:
  0.0 39.9 jit_solution(16501150988209285957)
XLA Ops:
  0.0 0.0 copy-start
  0.0 0.0 copy-start.1
  0.0 0.0 copy-start.2
  0.0 0.6 %copy-done = f32[64]{0:T(128)S(1)} copy-done((f32[64]{0:T(128)S(1)}, f32[64]{0:T(128)}, u32[]{:S(2)}) %copy-start) | copy-done | bytes 280
  0.7 0.0 copy-done.1
  0.7 0.0 copy-done.2
  0.7 0.6 %select_maximum_fusion.par_hbm = f32[8,128]{1,0:T(8,128)} fusion(f32[1,64]{1,0:T(1,128)S(1)} %bitcast.9, f32[1,64]{1,0:T(1,128)S(1)} %bitcast.10, f32[1,64]{1,0:T(1,128)S(1)} %bitcast.11), kind=kLoop, calls=%fused_computation | loop fusion | flops 11264 | bytes 4864 | tf_op jit(solution)/shard_map/stack | solution.py:361
  1.3 36.3 %shard_map.109 = bf16[1,128,4096]{2,1,0:T(8,128)(2,1)} custom-call(bf16[1,64,8192]{2,1,0:T(8,128)(2,1)} %x_ref.1, bf16[1,64,2048]{2,1,0:T(8,128)(2,1)} %bc_ref.1, bf16[1,64,128]{2,1,0:T(8,128)(2,1)} %dt_ref.1, f32[4,4096]{1,0:T(4,128)} %wx_hbm.1, f32[1,4096]{1,0:T(1,128)} %bitcast.6, f32[4,1024]{1,0:T(4,128)} %wb_hbm.1, f32[1,1024]{1,0:T(1,128)} %bitcast.8, ...), custom_call_target="tpu_custom_call" | custom-call | tf_op jit(solution)/shard_map/pallas_call | solution.py:365
  37.6 2.3 %copy.13 = bf16[1,128,4096]{2,1,0:T(8,128)(2,1)} copy(bf16[1,128,4096]{2,1,0:T(8,128)(2,1)} %shard_map.109) | data formatting | bytes 2097152
Async XLA Ops:
  0.0 0.7 %copy-start = (f32[64]{0:T(128)S(1)}, f32[64]{0:T(128)}, u32[]{:S(2)}) copy-start(f32[64]{0:T(128)} %param.20) | copy-start | bytes 772
  0.0 0.7 %copy-start.1 = (f32[64]{0:T(128)S(1)}, f32[64]{0:T(128)}, u32[]{:S(2)}) copy-start(f32[64]{0:T(128)} %param.19) | copy-start | bytes 772
  0.0 0.7 %copy-start.2 = (f32[64]{0:T(128)S(1)}, f32[64]{0:T(128)}, u32[]{:S(2)}) copy-start(f32[64]{0:T(128)} %param.18) | copy-start | bytes 772

commit v5 on v4

--- a/solution.py
+++ b/solution.py
@@ -21,7 +21,7 @@
 
 
 def kernel(nseq, nhead, x_ref, bc_ref, dt_ref, wx_hbm, bx_hbm, wb_hbm, bb_hbm, par_hbm, gain_hbm, out_ref,
-           wx_ref, bx_ref, wb_ref, bb_ref, par_ref, gain_ref, x_last, bc_last, par_l, x_l, b_l,
+           wx_ref, bx_ref, wb_ref, bb_ref, par_ref, gain_ref, x_last, bc_last, par_l, x_l, b_l, outv, o_l,
            xf, bcf, dtf, xc, bcc, ext, tail32, tail_out, tail_in, cum_sc, dt_sc, cumt_sc, dtt_sc, par_sc,
            end_out, end_in, st, sb, s0, ein, eout, cb, ysc, ecw,
            x_s, x_r, b_s, b_r, d_s, d_r, t_s, t_r, e_s, e_r, s_s, s_r, c_s, c_r, f_s, f_r):
@@ -302,6 +302,10 @@
     within(groups - 1)
     chain(groups + 1)
 
+    def out_copy(g):
+        at = pl.ds(pl.multiple_of(g * WIDE, WIDE), WIDE)
+        return pltpu.make_async_copy(outv.at[g], out_ref.at[0, :, at], o_l.at[g])
+
     def third(g, carry):
         chain(groups + 2 + g)
 
@@ -318,10 +322,13 @@
         y = y * ecw[g] + ysc[g]
         mean = jnp.mean(y * y, axis=1, keepdims=True)
         at = pl.ds(pl.multiple_of(g * WIDE, WIDE), WIDE)
-        out_ref[0, :, at] = (y * lax.rsqrt(mean + NORM_EPSILON) * gain_ref[:, at]).astype(BF16)
+        outv[g] = (y * lax.rsqrt(mean + NORM_EPSILON) * gain_ref[:, at]).astype(BF16)
+        out_copy(g).start()
         return carry
 
     lax.fori_loop(0, groups, third, 0)
+    for g in range(groups):
+        out_copy(g).wait()
 
     for d in range(nhead - 1):
         dt_copy(d).wait_send()
@@ -366,11 +373,11 @@
         functools.partial(kernel, nseq, nhead),
         out_shape=jax.ShapeDtypeStruct((1, SPAN, width), BF16),
         in_specs=[pl.BlockSpec(memory_space=pltpu.HBM)] * 9,
-        out_specs=pl.BlockSpec(memory_space=pltpu.VMEM),
+        out_specs=pl.BlockSpec(memory_space=pltpu.HBM),
         scratch_shapes=[
             V(conv_x_weight.shape, F32), V((1, width), F32), V(conv_bc_weight.shape, F32),
             V((1, conv_bc_weight.shape[1]), F32), V((8, 128), F32), V((1, width), F32),
-            V((16, x_raw.shape[2]), BF16), V((16, bc_raw.shape[2]), BF16), dma(9), dma(groups), dma(groups),
+            V((16, x_raw.shape[2]), BF16), V((16, bc_raw.shape[2]), BF16), dma(9), dma(groups), dma(groups), V(g3, BF16), dma(groups),
             V(g3, BF16), V((groups, SPAN, 2 * STATE), BF16), V((SPAN, 128), BF16),
             V(g3, BF16), V((groups, SPAN, 2 * STATE), BF16), V((SPAN + 8, WIDE + 2 * STATE), F32),
             V((16, WIDE), F32), V((nhead, 16, WIDE), BF16), V((16, WIDE), BF16),

time: 40.1 us -> 39.9 us (level); the launches traced: 39.9 us -> 39.2 us
  Pallas kernels: 36.3 us -> 35.6 us
    pallas_call x1, Pallas kernels: 36.3 us -> 35.6 us  [on_device(): pl.pallas_call(functools.partial(kernel, nseq, nhead), out_shape=jax.Shap...]
where the time goes in v5:
time: 39.9 us; the launch traced here: 39.2 us
  Pallas kernels  35.6 us (89%)
  local copies, waits for them, and re-layouts  2.97 us (7%)
  other arithmetic  0.6 us (2%)
    pallas_call x1, Pallas kernels, on_device(): pl.pallas_call(functools.partial(kernel, nseq, nhead), out_shape=jax.Shap...  35.6 us
    unnamed x7, local copies, waits for them, and re-layouts  2.97 us

profile of v5, /device:TPU:29, one launch (start us, length us, event | category | flops | bytes accessed | tf_op | source)
XLA Modules:
  0.0 39.2 jit_solution(9672857377055798256)
XLA Ops:
  0.0 0.0 copy-start
  0.0 0.0 copy-start.1
  0.0 0.0 copy-start.2
  0.0 0.6 %copy-done = f32[64]{0:T(128)S(1)} copy-done((f32[64]{0:T(128)S(1)}, f32[64]{0:T(128)}, u32[]{:S(2)}) %copy-start) | copy-done | bytes 280
  0.7 0.0 copy-done.1
  0.7 0.0 copy-done.2
  0.7 0.6 %select_maximum_fusion.par_hbm = f32[8,128]{1,0:T(8,128)} fusion(f32[1,64]{1,0:T(1,128)S(1)} %bitcast.9, f32[1,64]{1,0:T(1,128)S(1)} %bitcast.10, f32[1,64]{1,0:T(1,128)S(1)} %bitcast.11), kind=kLoop, calls=%fused_computation | loop fusion | flops 11264 | bytes 4864 | tf_op jit(solution)/shard_map/stack | solution.py:368
  1.3 35.6 %shard_map.109 = bf16[1,128,4096]{2,1,0:T(8,128)(2,1)} custom-call(bf16[1,64,8192]{2,1,0:T(8,128)(2,1)} %x_ref.1, bf16[1,64,2048]{2,1,0:T(8,128)(2,1)} %bc_ref.1, bf16[1,64,128]{2,1,0:T(8,128)(2,1)} %dt_ref.1, f32[4,4096]{1,0:T(4,128)} %wx_hbm.1, f32[1,4096]{1,0:T(1,128)} %bitcast.6, f32[4,1024]{1,0:T(4,128)} %wb_hbm.1, f32[1,1024]{1,0:T(1,128)} %bitcast.8, ...), custom_call_target="tpu_custom_call" | custom-call | tf_op jit(solution)/shard_map/pallas_call | solution.py:372
  36.9 2.3 %copy.13 = bf16[1,128,4096]{2,1,0:T(8,128)(2,1)} copy(bf16[1,128,4096]{2,1,0:T(8,128)(2,1)} %shard_map.109) | data formatting | bytes 2097152
Async XLA Ops:
  0.0 0.7 %copy-start = (f32[64]{0:T(128)S(1)}, f32[64]{0:T(128)}, u32[]{:S(2)}) copy-start(f32[64]{0:T(128)} %param.20) | copy-start | bytes 772
  0.0 0.7 %copy-start.1 = (f32[64]{0:T(128)S(1)}, f32[64]{0:T(128)}, u32[]{:S(2)}) copy-start(f32[64]{0:T(128)} %param.19) | copy-start | bytes 772
  0.0 0.7 %copy-start.2 = (f32[64]{0:T(128)S(1)}, f32[64]{0:T(128)}, u32[]{:S(2)}) copy-start(f32[64]{0:T(128)} %param.18) | copy-start | bytes 772
